TPU v7x, 32 devices: a whole 2x2x4 slice. The times are simulated.
32 devices in a mesh: slab: 16 (over z, y, core), plane: 2 (over x).
Axes of the slice: x: 2, y: 2, z: 4, core: 2. Of those that a mesh axis runs over, the one named last changes fastest.
Arguments:
- rock_state: float32 [2, 32, 16, 512], P(None, 'slab', 'plane'), may hold values from -6 to 6
- rock_source: float32 [2, 32, 16, 512], P(None, 'slab', 'plane'), may hold values from -6 to 6
- transmissibility: bfloat16 [3, 32, 16, 512], P(None, 'slab', 'plane'), may hold values from 0.039794922 to 0.29882812
- cell_inverse: bfloat16 [4, 32, 16, 512], P(None, 'slab', 'plane'), may hold values from -0.06 to 0.3
- fracture_state: float32 [2, 32768], P(None, ('slab', 'plane')), may hold values from -6 to 6
- fracture_source: float32 [2, 32768], P(None, ('slab', 'plane')), may hold values from -6 to 6
- fracture_coupling: bfloat16 [256, 3, 128, 128], P(('slab', 'plane')), may hold values from -0.25 to 0.25
- fracture_inverse: bfloat16 [256, 128, 128], P(('slab', 'plane')), may hold values from -0.044194174 to 0.3941942
- fracture_neighbours: int32 [256, 3], P(('slab', 'plane')), may hold values from 0 to 255, as said below
- contact_cell: int32 [16, 32, 128], P('slab', 'plane'), may hold values from 0 to 8191
- contact_segment: int32 [16, 32, 128], P('slab', 'plane'), may hold values from 0 to 1023
- contact_weight: float32 [16, 32, 128], P('slab', 'plane'), may hold values from 0.3 to 1.5
- contact_count: int32 [16, 32], P('slab', 'plane'), may hold values from 32 to 128, as said below
Outputs:
- rock_final: float32 [2, 32, 16, 512], P(None, 'slab', 'plane')
- fracture_final: float32 [2, 32768], P(None, ('slab', 'plane'))
Inputs may be any that keep to these rules, and one draw needn't show every extreme that they name: `contact_count`: live contact slots from one rock device to one fracture part of the same plane index; for every plane index some fracture part receives 128 live slots from every rock slab. `fracture_neighbours`: a block's neighbours are other blocks of its own part or of the parts one step away along slab with the same plane index.
All inputs are finite; a program needn't handle non-finite values.
Results may differ from a plain program's by a relative error of at most 0.0033.
Values may be sent and summed in bfloat16 or wider, within the bound.
A program may use at most 64 MiB of HBM per device.

v0:
```python
import jax
import jax.numpy as jnp
from jax import lax
from jax.sharding import PartitionSpec as P

ITERS = 3


def shifted(value, axis, steps):
    count = lax.axis_size(axis)
    first, last = (max(0, -steps), min(count, count - steps))
    return lax.ppermute(value, axis, [(source, source + steps) for source in range(first, last)])


def padded(block, sides, width):
    for axis, dim in sides:
        count = lax.axis_size(axis)
        forward = [(i, i + 1) for i in range(count - 1)]
        backward = [(target, source) for source, target in forward]
        low = lax.ppermute(
            lax.slice_in_dim(block, block.shape[dim] - width, None, axis=dim), axis, forward
        )
        high = lax.ppermute(lax.slice_in_dim(block, 0, width, axis=dim), axis, backward)
        block = jnp.concatenate([low, block, high], axis=dim)
    return block


def pick_values(row_onehot, col_mask, table):
    spread = jnp.einsum("kr,frc->fkc", row_onehot, table, precision=lax.Precision.HIGHEST)
    return jnp.sum(jnp.where(col_mask[None], spread, 0.0), axis=-1)


def place_values(row_onehot, col_mask, values):
    spread = jnp.where(col_mask[None], values[:, :, None], 0.0)
    return jnp.einsum("kr,fkc->frc", row_onehot, spread, precision=lax.Precision.HIGHEST)


def shards(
    rock_state,
    rock_source,
    transmissibility,
    cell_inverse,
    fracture_state,
    fracture_source,
    fracture_coupling,
    fracture_inverse,
    fracture_neighbours,
    contact_cell,
    contact_segment,
    contact_weight,
    contact_count,
):
    plane_count = lax.axis_size("plane")
    blocks = fracture_coupling.shape[0]
    segment_width = fracture_coupling.shape[-1]
    cell_table = contact_cell[0]
    slot_shape = cell_table.shape
    slot_index = lax.broadcasted_iota(jnp.int32, slot_shape, 1)
    slot_weight = jnp.where(slot_index < contact_count[0][:, None], contact_weight[0], 0.0)
    arrived_segment = lax.all_to_all(
        contact_segment[0], "slab", split_axis=0, concat_axis=0, tiled=True
    )
    my_part = lax.axis_index("slab") * plane_count + lax.axis_index("plane")
    owner_part = fracture_neighbours // blocks
    position = ((owner_part - my_part) // plane_count + 1) * blocks + fracture_neighbours % blocks
    rim_onehot = (
        position[:, :, None] == lax.broadcasted_iota(jnp.int32, (1, 1, 3 * blocks), 2)
    ).astype(jnp.bfloat16)
    cell_total = rock_state[0].size
    cell_rows = cell_total // 128
    cell_flat = cell_table.reshape(-1)
    cell_row_onehot = (
        (cell_flat // 128)[:, None] == lax.broadcasted_iota(jnp.int32, (1, cell_rows), 1)
    ).astype(jnp.float32)
    cell_col_mask = (cell_flat % 128)[:, None] == lax.broadcasted_iota(jnp.int32, (1, 128), 1)
    segment_flat = arrived_segment.reshape(-1)
    segment_row_onehot = (
        (segment_flat // segment_width)[:, None] == lax.broadcasted_iota(jnp.int32, (1, blocks), 1)
    ).astype(jnp.float32)
    segment_col_mask = (segment_flat % segment_width)[:, None] == lax.broadcasted_iota(
        jnp.int32, (1, segment_width), 1
    )
    coef_z = transmissibility[0]
    coef_x = transmissibility[1]
    coef_y = transmissibility[2]
    rock_now = rock_state
    fracture_now = fracture_state
    source_blocks = fracture_source.reshape(2, blocks, segment_width)
    for sweep_index in range(ITERS):
        rock_table = rock_now.reshape(2, cell_rows, 128)
        rock_picked = pick_values(cell_row_onehot, cell_col_mask, rock_table).reshape(
            (2,) + slot_shape
        )
        send_rock = slot_weight[None] * rock_picked
        fracture_table = fracture_now.reshape(2, blocks, segment_width)
        send_fracture = pick_values(segment_row_onehot, segment_col_mask, fracture_table).reshape(
            (2,) + slot_shape
        )
        got_rock, got_fracture = (
            lax.all_to_all(send_rock, "slab", split_axis=1, concat_axis=1, tiled=True),
            lax.all_to_all(send_fracture, "slab", split_axis=1, concat_axis=1, tiled=True),
        )
        leak_fracture = place_values(segment_row_onehot, segment_col_mask, got_rock.reshape(2, -1))
        leak_rock = place_values(
            cell_row_onehot, cell_col_mask, (slot_weight[None] * got_fracture).reshape(2, -1)
        ).reshape(rock_now.shape)
        fracture_low = fracture_now.astype(jnp.bfloat16).reshape(2, blocks, segment_width)
        fracture_padded = padded(fracture_low, (("slab", 1),), blocks)
        gathered = jnp.einsum(
            "bkq,fqj->fbkj", rim_onehot, fracture_padded, preferred_element_type=jnp.float32
        ).astype(jnp.bfloat16)
        coupled = jnp.einsum(
            "bkij,fbkj->fbi", fracture_coupling, gathered, preferred_element_type=jnp.float32
        )
        fracture_rhs = (source_blocks + leak_fracture - coupled).astype(jnp.bfloat16)
        fracture_next = jnp.einsum(
            "bij,fbj->fbi", fracture_inverse, fracture_rhs, preferred_element_type=jnp.float32
        ).reshape(2, -1)
        y_product = coef_y * rock_now
        total = coef_y * jnp.pad(rock_now[..., :-1], ((0, 0), (0, 0), (0, 0), (1, 0)))
        total = total + jnp.pad(y_product[..., 1:], ((0, 0), (0, 0), (0, 0), (0, 1)))
        z_product = coef_z * rock_now
        x_product = coef_x * rock_now
        from_below = shifted(rock_now[:, -1:], "slab", 1)
        from_above = shifted(z_product[:, :1], "slab", -1)
        from_left = shifted(rock_now[:, :, -1:], "plane", 1)
        from_right = shifted(x_product[:, :, :1], "plane", -1)
        total = (
            total
            + coef_z * jnp.concatenate([from_below, rock_now[:, :-1]], 1)
            + jnp.concatenate([z_product[:, 1:], from_above], 1)
        )
        total = (
            total
            + coef_x * jnp.concatenate([from_left, rock_now[:, :, :-1]], 2)
            + jnp.concatenate([x_product[:, :, 1:], from_right], 2)
        )
        rock_rhs = rock_source + total + leak_rock
        rock_now = jnp.stack(
            [
                cell_inverse[0] * rock_rhs[0] + cell_inverse[1] * rock_rhs[1],
                cell_inverse[2] * rock_rhs[0] + cell_inverse[3] * rock_rhs[1],
            ]
        )
        fracture_now = fracture_next
    return (rock_now, fracture_now)


def solution(mesh):
    return jax.shard_map(
        shards,
        mesh=mesh,
        in_specs=(
            P(None, "slab", "plane", None),
            P(None, "slab", "plane", None),
            P(None, "slab", "plane", None),
            P(None, "slab", "plane", None),
            P(None, ("slab", "plane")),
            P(None, ("slab", "plane")),
            P(("slab", "plane"), None, None, None),
            P(("slab", "plane"), None, None),
            P(("slab", "plane"), None),
            P("slab", "plane", None),
            P("slab", "plane", None),
            P("slab", "plane", None),
            P("slab", "plane"),
        ),
        out_specs=(P(None, "slab", "plane", None), P(None, ("slab", "plane"))),
        check_vma=False,
    )
```

profile of v0, /device:TPU:0, one launch (start us, length us, event | category | flops | bytes accessed | tf_op | source)
XLA Modules:
  0.0 132.2 jit_solution(17171232244759082843)
XLA Ops:
  2.8 3.0 %collective-permute-start.8 = (bf16[2,8,128]{2,1,0:T(8,128)(2,1)S(1)}, bf16[2,8,128]{2,1,0:T(8,128)(2,1)S(1)}, u32[]{:S(2)}, u32[]{:S(2)}) collective-permute-start(bf16[2,8,128]{2,1,0:T(8,128)(2,1)S(1)} %bitcast.239), channel_id=1, source_target_pairs={{0,2},{2,4},{4,6},{6,8},{8,10},{10,12},{12,14},{14,16},{16,18},{18... | collective-permute-start | bytes 12296 | tf_op jit(solution)/shard_map/ppermute | solution.py:20
  5.8 8.0 %all-to-all-start = ((s32[16,1,128]{2,1,0:T(1,128)}), s32[16,1,128]{2,1,0:T(1,128)S(1)}, u32[]{:S(2)}, u32[]{:S(2)}) async-start(s32[16,1,128]{2,1,0:T(1,128)} %bitcast.237), calls=%async_computation | async-start | bytes 16384 | tf_op jit(solution)/shard_map/all_to_all | solution.py:60
  14.6 2.3 %collective-permute-start = (f32[2,1,8,512]{3,2,1,0:T(8,128)S(1)}, f32[2,1,8,512]{3,2,1,0:T(8,128)S(1)}, u32[]{:S(2)}, u32[]{:S(2)}) collective-permute-start(f32[2,1,8,512]{3,2,1,0:T(8,128)S(1)} %get-tuple-element.30), channel_id=1, source_target_pairs={{0,2},{2,4},{4,6},{6,8},{8,10},{10,12},{12,14},{14,16},{16,18},{18... | collective-permute-start | bytes 98312 | tf_op jit(solution)/shard_map/ppermute | solution.py:12
  20.6 3.4 %collective-permute-start.2 = (f32[2,2,1,512]{3,2,1,0:T(1,128)S(1)}, f32[2,2,1,512]{3,2,1,0:T(1,128)S(1)}, u32[]{:S(2)}, u32[]{:S(2)}) collective-permute-start(f32[2,2,1,512]{3,2,1,0:T(1,128)S(1)} %slice.153), channel_id=1, source_target_pairs={{0,1},{2,3},{4,5},{6,7},{8,9},{10,11},{12,13},{14,15},{16,17},{18,... | collective-permute-start | bytes 24584 | tf_op jit(solution)/shard_map/ppermute | solution.py:12
  27.8 8.0 %all-to-all-start.2 = ((f32[2,16,128]{2,0,1:T(2,128)}), f32[2,16,128]{2,0,1:T(2,128)S(1)}, u32[]{:S(2)}, u32[]{:S(2)}) async-start(f32[2,16,128]{2,0,1:T(2,128)} %copy.36), calls=%async_computation.2 | async-start | bytes 32768 | tf_op jit(solution)/shard_map/all_to_all | solution.py:100
  36.0 1.8 %select_reduce_fusion = f32[2048,2]{0,1:T(2,128)} fusion(pred[2048,128]{0,1:T(8,128)(4,1)S(1)} %iota_compare_fusion, f32[1,2,8,128]{3,1,2,0:T(2,128)S(1)} %bitcast.228, s32[2048]{0:T(1024)S(1)} %get-tuple-element.41), kind=kOutput, calls=%fused_computation.21 | convolution fusion | flops 51392512 | bytes 294912
  37.8 4.5 %all-to-all-done.2 = f32[2,16,128]{2,0,1:T(2,128)S(1)} async-done(((f32[2,16,128]{2,0,1:T(2,128)}), f32[2,16,128]{2,0,1:T(2,128)S(1)}, u32[]{:S(2)}, u32[]{:S(2)}) %all-to-all-start.2) | async-done | bytes 16416 | tf_op jit(solution)/shard_map/all_to_all | solution.py:100
  42.3 3.6 %all-to-all-start.1 = ((f32[2,16,128]{2,0,1:T(2,128)}), f32[2,16,128]{2,0,1:T(2,128)S(1)}, u32[]{:S(2)}, u32[]{:S(2)}) async-start(f32[2,16,128]{2,0,1:T(2,128)} %bitcast.13), calls=%async_computation.1 | async-start | bytes 32768 | tf_op jit(solution)/shard_map/all_to_all | solution.py:101
  48.8 3.0 %collective-permute-start.14 = (bf16[2,8,128]{2,0,1:T(2,128)(2,1)S(1)}, bf16[2,8,128]{2,0,1:T(2,128)(2,1)S(1)}, u32[]{:S(2)}, u32[]{:S(2)}) collective-permute-start(bf16[2,8,128]{2,0,1:T(2,128)(2,1)S(1)} %get-tuple-element.43), channel_id=1, source_target_pairs={{0,2},{2,4},{4,6},{6,8},{8,10},{10,12},{12,14},{14,16},{16,18},{18... | collective-permute-start | bytes 12296 | tf_op jit(solution)/shard_map/ppermute | solution.py:20
  51.8 1.8 %fusion.19 = f32[2,2048]{1,0:T(2,128)} fusion(pred[2048,128]{0,1:T(8,128)(4,1)S(1)} %iota_compare_fusion, s32[2048]{0:T(1024)S(1)} %get-tuple-element.41, f32[2,8,128]{2,0,1:T(2,128)S(1)} %get-tuple-element.44), kind=kOutput, calls=%fused_computation.25 | convolution fusion | flops 51392512 | bytes 294912 | tf_op jit(solution)/shard_map/kr,frc->fkc/dot_general | solution.py:29
  55.1 6.9 %all-to-all-start.3 = ((f32[2,16,128]{2,0,1:T(2,128)}), f32[2,16,128]{2,0,1:T(2,128)S(1)}, u32[]{:S(2)}, u32[]{:S(2)}) async-start(f32[2,16,128]{2,0,1:T(2,128)} %bitcast.29), calls=%async_computation.3 | async-start | bytes 32768 | tf_op jit(solution)/shard_map/all_to_all | solution.py:101
  62.4 6.1 %all-to-all-done.3 = f32[2,16,128]{2,0,1:T(2,128)S(1)} async-done(((f32[2,16,128]{2,0,1:T(2,128)}), f32[2,16,128]{2,0,1:T(2,128)S(1)}, u32[]{:S(2)}, u32[]{:S(2)}) %all-to-all-start.3) | async-done | bytes 16416 | tf_op jit(solution)/shard_map/all_to_all | solution.py:101
  72.5 1.7 %collective-permute-start.4 = (f32[2,1,8,512]{3,2,1,0:T(8,128)S(1)}, f32[2,1,8,512]{3,2,1,0:T(8,128)S(1)}, u32[]{:S(2)}, u32[]{:S(2)}) collective-permute-start(f32[2,1,8,512]{3,2,1,0:T(8,128)S(1)} %get-tuple-element.22), channel_id=1, source_target_pairs={{0,2},{2,4},{4,6},{6,8},{8,10},{10,12},{12,14},{14,16},{16,18},{18... | collective-permute-start | bytes 98312 | tf_op jit(solution)/shard_map/ppermute | solution.py:12
  75.4 4.3 %collective-permute-start.6 = (f32[2,2,1,512]{3,2,1,0:T(1,128)S(1)}, f32[2,2,1,512]{3,2,1,0:T(1,128)S(1)}, u32[]{:S(2)}, u32[]{:S(2)}) collective-permute-start(f32[2,2,1,512]{3,2,1,0:T(1,128)S(1)} %fusion.176), channel_id=1, source_target_pairs={{0,1},{2,3},{4,5},{6,7},{8,9},{10,11},{12,13},{14,15},{16,17},{18,... | collective-permute-start | bytes 24584 | tf_op jit(solution)/shard_map/ppermute | solution.py:12
  79.7 1.5 %collective-permute-start.7 = (f32[2,2,1,512]{3,2,1,0:T(1,128)S(1)}, f32[2,2,1,512]{3,2,1,0:T(1,128)S(1)}, u32[]{:S(2)}, u32[]{:S(2)}) collective-permute-start(f32[2,2,1,512]{3,2,1,0:T(1,128)S(1)} %slice.210), channel_id=1, source_target_pairs={{1,0},{3,2},{5,4},{7,6},{9,8},{11,10},{13,12},{15,14},{17,16},{19,... | collective-permute-start | bytes 24584 | tf_op jit(solution)/shard_map/ppermute | solution.py:12
  82.5 2.8 %collective-permute-done.7 = f32[2,2,1,512]{3,2,1,0:T(1,128)S(1)} collective-permute-done((f32[2,2,1,512]{3,2,1,0:T(1,128)S(1)}, f32[2,2,1,512]{3,2,1,0:T(1,128)S(1)}, u32[]{:S(2)}, u32[]{:S(2)}) %collective-permute-start.7) | collective-permute-done | bytes 8224 | tf_op jit(solution)/shard_map/ppermute | solution.py:12
  87.5 5.4 %all-to-all-start.4 = ((f32[2,16,128]{2,0,1:T(2,128)}), f32[2,16,128]{2,0,1:T(2,128)S(1)}, u32[]{:S(2)}, u32[]{:S(2)}) async-start(f32[2,16,128]{2,0,1:T(2,128)} %copy.44), calls=%async_computation.4 | async-start | bytes 32768 | tf_op jit(solution)/shard_map/all_to_all | solution.py:100
  92.9 2.3 %collective-permute-start.10 = (f32[2,1,8,512]{3,2,1,0:T(8,128)S(1)}, f32[2,1,8,512]{3,2,1,0:T(8,128)S(1)}, u32[]{:S(2)}, u32[]{:S(2)}) collective-permute-start(f32[2,1,8,512]{3,2,1,0:T(8,128)S(1)} %get-tuple-element.14), channel_id=1, source_target_pairs={{0,2},{2,4},{4,6},{6,8},{8,10},{10,12},{12,14},{14,16},{16,18},{18... | collective-permute-start | bytes 98312 | tf_op jit(solution)/shard_map/ppermute | solution.py:12
  96.5 1.8 %collective-permute-start.12 = (f32[2,2,1,512]{3,2,1,0:T(1,128)S(1)}, f32[2,2,1,512]{3,2,1,0:T(1,128)S(1)}, u32[]{:S(2)}, u32[]{:S(2)}) collective-permute-start(f32[2,2,1,512]{3,2,1,0:T(1,128)S(1)} %fusion.175), channel_id=1, source_target_pairs={{0,1},{2,3},{4,5},{6,7},{8,9},{10,11},{12,13},{14,15},{16,17},{18,... | collective-permute-start | bytes 24584 | tf_op jit(solution)/shard_map/ppermute | solution.py:12
  99.4 7.5 %all-to-all-start.6 = ((f32[2,16,128]{2,0,1:T(2,128)}), f32[2,16,128]{2,0,1:T(2,128)S(1)}, u32[]{:S(2)}, u32[]{:S(2)}) async-start(f32[2,16,128]{2,0,1:T(2,128)} %copy.53), calls=%async_computation.6 | async-start | bytes 32768 | tf_op jit(solution)/shard_map/all_to_all | solution.py:100
  109.7 3.0 %collective-permute-start.16 = (bf16[2,8,128]{2,0,1:T(2,128)(2,1)S(1)}, bf16[2,8,128]{2,0,1:T(2,128)(2,1)S(1)}, u32[]{:S(2)}, u32[]{:S(2)}) collective-permute-start(bf16[2,8,128]{2,0,1:T(2,128)(2,1)S(1)} %get-tuple-element.45), channel_id=1, source_target_pairs={{0,2},{2,4},{4,6},{6,8},{8,10},{10,12},{12,14},{14,16},{16,18},{18... | collective-permute-start | bytes 12296 | tf_op jit(solution)/shard_map/ppermute | solution.py:20
  112.7 1.8 %fusion.20 = f32[2,2048]{1,0:T(2,128)} fusion(pred[2048,128]{0,1:T(8,128)(4,1)S(1)} %iota_compare_fusion, s32[2048]{0:T(1024)S(1)} %get-tuple-element.41, f32[2,8,128]{2,0,1:T(2,128)S(1)} %get-tuple-element.46), kind=kOutput, calls=%fused_computation.26 | convolution fusion | flops 51392512 | bytes 294912 | tf_op jit(solution)/shard_map/kr,frc->fkc/dot_general | solution.py:29
  116.4 7.0 %all-to-all-start.5 = ((f32[2,16,128]{2,0,1:T(2,128)}), f32[2,16,128]{2,0,1:T(2,128)S(1)}, u32[]{:S(2)}, u32[]{:S(2)}) async-start(f32[2,16,128]{2,0,1:T(2,128)} %bitcast.41), calls=%async_computation.5 | async-start | bytes 32768 | tf_op jit(solution)/shard_map/all_to_all | solution.py:101
  125.6 4.4 %all-to-all-done.5 = f32[2,16,128]{2,0,1:T(2,128)S(1)} async-done(((f32[2,16,128]{2,0,1:T(2,128)}), f32[2,16,128]{2,0,1:T(2,128)S(1)}, u32[]{:S(2)}, u32[]{:S(2)}) %all-to-all-start.5) | async-done | bytes 16416 | tf_op jit(solution)/shard_map/all_to_all | solution.py:101
  (128 shorter events, 34.9 us)
Async XLA Ops:
  1.5 25.8 %collective-permute-start.9 = (bf16[2,8,128]{2,1,0:T(8,128)(2,1)S(1)}, bf16[2,8,128]{2,1,0:T(8,128)(2,1)S(1)}, u32[]{:S(2)}, u32[]{:S(2)}) collective-permute-start(bf16[2,8,128]{2,1,0:T(8,128)(2,1)S(1)} %bitcast.238), channel_id=1, source_target_pairs={{2,0},{4,2},{6,4},{8,6},{10,8},{12,10},{14,12},{16,14},{18,16},{20... | collective-permute-start | bytes 12296 | tf_op jit(solution)/shard_map/ppermute | solution.py:23
  2.8 24.5 %collective-permute-start.8 = (bf16[2,8,128]{2,1,0:T(8,128)(2,1)S(1)}, bf16[2,8,128]{2,1,0:T(8,128)(2,1)S(1)}, u32[]{:S(2)}, u32[]{:S(2)}) collective-permute-start(bf16[2,8,128]{2,1,0:T(8,128)(2,1)S(1)} %bitcast.239), channel_id=1, source_target_pairs={{0,2},{2,4},{4,6},{6,8},{8,10},{10,12},{12,14},{14,16},{16,18},{18... | collective-permute-start | bytes 12296 | tf_op jit(solution)/shard_map/ppermute | solution.py:20
  5.8 22.0 %all-to-all-start = ((s32[16,1,128]{2,1,0:T(1,128)}), s32[16,1,128]{2,1,0:T(1,128)S(1)}, u32[]{:S(2)}, u32[]{:S(2)}) async-start(s32[16,1,128]{2,1,0:T(1,128)} %bitcast.237), calls=%async_computation | async-start | bytes 16384 | tf_op jit(solution)/shard_map/all_to_all | solution.py:60
  14.6 55.5 %collective-permute-start = (f32[2,1,8,512]{3,2,1,0:T(8,128)S(1)}, f32[2,1,8,512]{3,2,1,0:T(8,128)S(1)}, u32[]{:S(2)}, u32[]{:S(2)}) collective-permute-start(f32[2,1,8,512]{3,2,1,0:T(8,128)S(1)} %get-tuple-element.30), channel_id=1, source_target_pairs={{0,2},{2,4},{4,6},{6,8},{8,10},{10,12},{12,14},{14,16},{16,18},{18... | collective-permute-start | bytes 98312 | tf_op jit(solution)/shard_map/ppermute | solution.py:12
  18.5 51.6 %collective-permute-start.1 = (f32[2,1,8,512]{3,2,1,0:T(8,128)S(1)}, f32[2,1,8,512]{3,2,1,0:T(8,128)S(1)}, u32[]{:S(2)}, u32[]{:S(2)}) collective-permute-start(f32[2,1,8,512]{3,2,1,0:T(8,128)S(1)} %get-tuple-element.29), channel_id=1, source_target_pairs={{2,0},{4,2},{6,4},{8,6},{10,8},{12,10},{14,12},{16,14},{18,16},{20... | collective-permute-start | bytes 98312 | tf_op jit(solution)/shard_map/ppermute | solution.py:12
  20.6 49.4 %collective-permute-start.2 = (f32[2,2,1,512]{3,2,1,0:T(1,128)S(1)}, f32[2,2,1,512]{3,2,1,0:T(1,128)S(1)}, u32[]{:S(2)}, u32[]{:S(2)}) collective-permute-start(f32[2,2,1,512]{3,2,1,0:T(1,128)S(1)} %slice.153), channel_id=1, source_target_pairs={{0,1},{2,3},{4,5},{6,7},{8,9},{10,11},{12,13},{14,15},{16,17},{18,... | collective-permute-start | bytes 24584 | tf_op jit(solution)/shard_map/ppermute | solution.py:12
  27.8 14.5 %all-to-all-start.2 = ((f32[2,16,128]{2,0,1:T(2,128)}), f32[2,16,128]{2,0,1:T(2,128)S(1)}, u32[]{:S(2)}, u32[]{:S(2)}) async-start(f32[2,16,128]{2,0,1:T(2,128)} %copy.36), calls=%async_computation.2 | async-start | bytes 32768 | tf_op jit(solution)/shard_map/all_to_all | solution.py:100
  42.3 12.8 %all-to-all-start.1 = ((f32[2,16,128]{2,0,1:T(2,128)}), f32[2,16,128]{2,0,1:T(2,128)S(1)}, u32[]{:S(2)}, u32[]{:S(2)}) async-start(f32[2,16,128]{2,0,1:T(2,128)} %bitcast.13), calls=%async_computation.1 | async-start | bytes 32768 | tf_op jit(solution)/shard_map/all_to_all | solution.py:101
  47.4 6.2 %collective-permute-start.15 = (bf16[2,8,128]{2,0,1:T(2,128)(2,1)S(1)}, bf16[2,8,128]{2,0,1:T(2,128)(2,1)S(1)}, u32[]{:S(2)}, u32[]{:S(2)}) collective-permute-start(bf16[2,8,128]{2,0,1:T(2,128)(2,1)S(1)} %get-tuple-element.43), channel_id=1, source_target_pairs={{2,0},{4,2},{6,4},{8,6},{10,8},{12,10},{14,12},{16,14},{18,16},{20... | collective-permute-start | bytes 12296 | tf_op jit(solution)/shard_map/ppermute | solution.py:23
  48.8 6.1 %collective-permute-start.14 = (bf16[2,8,128]{2,0,1:T(2,128)(2,1)S(1)}, bf16[2,8,128]{2,0,1:T(2,128)(2,1)S(1)}, u32[]{:S(2)}, u32[]{:S(2)}) collective-permute-start(bf16[2,8,128]{2,0,1:T(2,128)(2,1)S(1)} %get-tuple-element.43), channel_id=1, source_target_pairs={{0,2},{2,4},{4,6},{6,8},{8,10},{10,12},{12,14},{14,16},{16,18},{18... | collective-permute-start | bytes 12296 | tf_op jit(solution)/shard_map/ppermute | solution.py:20
  53.6 16.5 %collective-permute-start.3 = (f32[2,2,1,512]{3,2,1,0:T(1,128)S(1)}, f32[2,2,1,512]{3,2,1,0:T(1,128)S(1)}, u32[]{:S(2)}, u32[]{:S(2)}) collective-permute-start(f32[2,2,1,512]{3,2,1,0:T(1,128)S(1)} %slice.191), channel_id=1, source_target_pairs={{1,0},{3,2},{5,4},{7,6},{9,8},{11,10},{13,12},{15,14},{17,16},{19,... | collective-permute-start | bytes 24584 | tf_op jit(solution)/shard_map/ppermute | solution.py:12
  55.1 13.4 %all-to-all-start.3 = ((f32[2,16,128]{2,0,1:T(2,128)}), f32[2,16,128]{2,0,1:T(2,128)S(1)}, u32[]{:S(2)}, u32[]{:S(2)}) async-start(f32[2,16,128]{2,0,1:T(2,128)} %bitcast.29), calls=%async_computation.3 | async-start | bytes 32768 | tf_op jit(solution)/shard_map/all_to_all | solution.py:101
  72.5 12.8 %collective-permute-start.4 = (f32[2,1,8,512]{3,2,1,0:T(8,128)S(1)}, f32[2,1,8,512]{3,2,1,0:T(8,128)S(1)}, u32[]{:S(2)}, u32[]{:S(2)}) collective-permute-start(f32[2,1,8,512]{3,2,1,0:T(8,128)S(1)} %get-tuple-element.22), channel_id=1, source_target_pairs={{0,2},{2,4},{4,6},{6,8},{8,10},{10,12},{12,14},{14,16},{16,18},{18... | collective-permute-start | bytes 98312 | tf_op jit(solution)/shard_map/ppermute | solution.py:12
  74.1 11.1 %collective-permute-start.5 = (f32[2,1,8,512]{3,2,1,0:T(8,128)S(1)}, f32[2,1,8,512]{3,2,1,0:T(8,128)S(1)}, u32[]{:S(2)}, u32[]{:S(2)}) collective-permute-start(f32[2,1,8,512]{3,2,1,0:T(8,128)S(1)} %get-tuple-element.21), channel_id=1, source_target_pairs={{2,0},{4,2},{6,4},{8,6},{10,8},{12,10},{14,12},{16,14},{18,16},{20... | collective-permute-start | bytes 98312 | tf_op jit(solution)/shard_map/ppermute | solution.py:12
  75.4 7.0 %collective-permute-start.6 = (f32[2,2,1,512]{3,2,1,0:T(1,128)S(1)}, f32[2,2,1,512]{3,2,1,0:T(1,128)S(1)}, u32[]{:S(2)}, u32[]{:S(2)}) collective-permute-start(f32[2,2,1,512]{3,2,1,0:T(1,128)S(1)} %fusion.176), channel_id=1, source_target_pairs={{0,1},{2,3},{4,5},{6,7},{8,9},{10,11},{12,13},{14,15},{16,17},{18,... | collective-permute-start | bytes 24584 | tf_op jit(solution)/shard_map/ppermute | solution.py:12
  87.5 11.9 %all-to-all-start.4 = ((f32[2,16,128]{2,0,1:T(2,128)}), f32[2,16,128]{2,0,1:T(2,128)S(1)}, u32[]{:S(2)}, u32[]{:S(2)}) async-start(f32[2,16,128]{2,0,1:T(2,128)} %copy.44), calls=%async_computation.4 | async-start | bytes 32768 | tf_op jit(solution)/shard_map/all_to_all | solution.py:100
  92.9 38.5 %collective-permute-start.10 = (f32[2,1,8,512]{3,2,1,0:T(8,128)S(1)}, f32[2,1,8,512]{3,2,1,0:T(8,128)S(1)}, u32[]{:S(2)}, u32[]{:S(2)}) collective-permute-start(f32[2,1,8,512]{3,2,1,0:T(8,128)S(1)} %get-tuple-element.14), channel_id=1, source_target_pairs={{0,2},{2,4},{4,6},{6,8},{8,10},{10,12},{12,14},{14,16},{16,18},{18... | collective-permute-start | bytes 98312 | tf_op jit(solution)/shard_map/ppermute | solution.py:12
  95.2 36.2 %collective-permute-start.11 = (f32[2,1,8,512]{3,2,1,0:T(8,128)S(1)}, f32[2,1,8,512]{3,2,1,0:T(8,128)S(1)}, u32[]{:S(2)}, u32[]{:S(2)}) collective-permute-start(f32[2,1,8,512]{3,2,1,0:T(8,128)S(1)} %get-tuple-element.13), channel_id=1, source_target_pairs={{2,0},{4,2},{6,4},{8,6},{10,8},{12,10},{14,12},{16,14},{18,16},{20... | collective-permute-start | bytes 98312 | tf_op jit(solution)/shard_map/ppermute | solution.py:12
  96.5 34.9 %collective-permute-start.12 = (f32[2,2,1,512]{3,2,1,0:T(1,128)S(1)}, f32[2,2,1,512]{3,2,1,0:T(1,128)S(1)}, u32[]{:S(2)}, u32[]{:S(2)}) collective-permute-start(f32[2,2,1,512]{3,2,1,0:T(1,128)S(1)} %fusion.175), channel_id=1, source_target_pairs={{0,1},{2,3},{4,5},{6,7},{8,9},{10,11},{12,13},{14,15},{16,17},{18,... | collective-permute-start | bytes 24584 | tf_op jit(solution)/shard_map/ppermute | solution.py:12
  99.4 17.0 %all-to-all-start.6 = ((f32[2,16,128]{2,0,1:T(2,128)}), f32[2,16,128]{2,0,1:T(2,128)S(1)}, u32[]{:S(2)}, u32[]{:S(2)}) async-start(f32[2,16,128]{2,0,1:T(2,128)} %copy.53), calls=%async_computation.6 | async-start | bytes 32768 | tf_op jit(solution)/shard_map/all_to_all | solution.py:100
  108.4 6.2 %collective-permute-start.17 = (bf16[2,8,128]{2,0,1:T(2,128)(2,1)S(1)}, bf16[2,8,128]{2,0,1:T(2,128)(2,1)S(1)}, u32[]{:S(2)}, u32[]{:S(2)}) collective-permute-start(bf16[2,8,128]{2,0,1:T(2,128)(2,1)S(1)} %get-tuple-element.45), channel_id=1, source_target_pairs={{2,0},{4,2},{6,4},{8,6},{10,8},{12,10},{14,12},{16,14},{18,16},{20... | collective-permute-start | bytes 12296 | tf_op jit(solution)/shard_map/ppermute | solution.py:23
  109.7 6.1 %collective-permute-start.16 = (bf16[2,8,128]{2,0,1:T(2,128)(2,1)S(1)}, bf16[2,8,128]{2,0,1:T(2,128)(2,1)S(1)}, u32[]{:S(2)}, u32[]{:S(2)}) collective-permute-start(bf16[2,8,128]{2,0,1:T(2,128)(2,1)S(1)} %get-tuple-element.45), channel_id=1, source_target_pairs={{0,2},{2,4},{4,6},{6,8},{8,10},{10,12},{12,14},{14,16},{16,18},{18... | collective-permute-start | bytes 12296 | tf_op jit(solution)/shard_map/ppermute | solution.py:20
  114.5 16.9 %collective-permute-start.13 = (f32[2,2,1,512]{3,2,1,0:T(1,128)S(1)}, f32[2,2,1,512]{3,2,1,0:T(1,128)S(1)}, u32[]{:S(2)}, u32[]{:S(2)}) collective-permute-start(f32[2,2,1,512]{3,2,1,0:T(1,128)S(1)} %slice.229), channel_id=1, source_target_pairs={{1,0},{3,2},{5,4},{7,6},{9,8},{11,10},{13,12},{15,14},{17,16},{19,... | collective-permute-start | bytes 24584 | tf_op jit(solution)/shard_map/ppermute | solution.py:12
  116.4 13.5 %all-to-all-start.5 = ((f32[2,16,128]{2,0,1:T(2,128)}), f32[2,16,128]{2,0,1:T(2,128)S(1)}, u32[]{:S(2)}, u32[]{:S(2)}) async-start(f32[2,16,128]{2,0,1:T(2,128)} %bitcast.41), calls=%async_computation.5 | async-start | bytes 32768 | tf_op jit(solution)/shard_map/all_to_all | solution.py:101
  (12 other events, 167.4 us)
where the time goes:
time: 133 us; the launch traced here: 132 us
  starting transfers between devices  83 us (62%)
  matrix products  20 us (15%)
  waiting for transfers between devices  18.4 us (14%)
  local copies, waits for them, and re-layouts  5.27 us (4%)
  other arithmetic  4.18 us (3%)
  between operations  1.4 us (1%)
    ppermute x12, starting transfers between devices, shifted(): lax.ppermute(value, axis, [(source, source + steps) for source in range(f...  23.6 us
    all_to_all x3, starting transfers between devices, shards(): lax.all_to_all(send_rock, 'slab', split_axis=1, concat_axis=1, tiled=True)  20.9 us
    all_to_all x3, starting transfers between devices, shards(): lax.all_to_all(send_fracture, 'slab', split_axis=1, concat_axis=1, tiled=...  17.6 us
    all_to_all x3, waiting for transfers between devices, shards(): lax.all_to_all(send_fracture, 'slab', split_axis=1, concat_axis=1, tiled=...  10.5 us
    ppermute x3, starting transfers between devices, padded(): lax.ppermute(lax.slice_in_dim(block, block.shape[dim] - width, None, axis...  9.09 us
    all_to_all x1, starting transfers between devices, shards(): lax.all_to_all(contact_segment[0], 'slab', split_axis=0, concat_axis=0, t...  7.96 us
    dot_general x6, matrix products, place_values(): jnp.einsum('kr,fkc->frc', row_onehot, spread, precision=lax.Precision.HIG...  7.96 us
    dot_general x5, matrix products, pick_values(): jnp.einsum('kr,frc->fkc', row_onehot, table, precision=lax.Precision.HIGH...  7.24 us
  transfers between devices with their start and end apart: 25, of which 5 were waited for; matrix products, arithmetic and copies ran while one was open for 18% of the time, Pallas kernels for 0%

commit v1 on v0

v1 whole, which is shorter than its diff:
```python
import functools

import jax
import jax.numpy as jnp
from jax import lax
from jax.experimental import pallas as pl
from jax.experimental.pallas import tpu as pltpu
from jax.sharding import PartitionSpec as P

ITERS = 3
LANES = 128
F32 = jnp.float32
BF16 = jnp.bfloat16
MESH = pl.DeviceIdType.MESH
NT = (((1,), (1,)), ((), ()))


def split(value):
    high = value.astype(BF16)
    low = (value - high.astype(F32)).astype(BF16)
    return high, low


def kernel(
    n,
    planes,
    rock_ref,
    source_ref,
    trans_ref,
    inverse_ref,
    frac_ref,
    frac_source_ref,
    coupling_ref,
    frac_inverse_ref,
    near_ref,
    cell_ref,
    segment_ref,
    weight_ref,
    count_ref,
    rock_out,
    frac_out,
    cell_hot,
    cell_mask,
    seg_hot,
    seg_mask,
    weights,
    seg_send,
    seg_recv,
    slot_send,
    slot_recv,
    up_send,
    down_send,
    up_recv,
    down_recv,
    right_send,
    left_send,
    right_recv,
    left_recv,
    frac_send,
    below_recv,
    above_recv,
    seg_sems,
    slot_sems,
    halo_send_sems,
    halo_recv_sems,
):
    slab = lax.axis_index("slab")
    plane = lax.axis_index("plane")
    blocks = coupling_ref.shape[0]
    has_below, has_above = slab > 0, slab < n - 1
    has_left, has_right = plane > 0, plane < planes - 1

    barrier = pltpu.get_barrier_semaphore()

    def greet(step, carry):
        pl.semaphore_signal(
            barrier, inc=1, device_id={"slab": lax.rem(slab + step, n)}, device_id_type=MESH
        )
        return carry

    lax.fori_loop(1, n, greet, 0)

    @pl.when(has_left)
    def _():
        pl.semaphore_signal(barrier, inc=1, device_id={"plane": plane - 1}, device_id_type=MESH)

    @pl.when(has_right)
    def _():
        pl.semaphore_signal(barrier, inc=1, device_id={"plane": plane + 1}, device_id_type=MESH)

    for s in range(n):
        seg_send[s] = segment_ref[0, s : s + 1, :]

    @pl.when(jnp.logical_not(has_below))
    def _():
        up_recv[...] = jnp.zeros_like(up_recv)
        below_recv[...] = jnp.zeros_like(below_recv)

    @pl.when(jnp.logical_not(has_above))
    def _():
        down_recv[...] = jnp.zeros_like(down_recv)
        above_recv[...] = jnp.zeros_like(above_recv)

    @pl.when(jnp.logical_not(has_left))
    def _():
        right_recv[...] = jnp.zeros_like(right_recv)

    @pl.when(jnp.logical_not(has_right))
    def _():
        left_recv[...] = jnp.zeros_like(left_recv)

    neighbours_x = has_left.astype(jnp.int32) + has_right.astype(jnp.int32)
    pl.semaphore_wait(barrier, n - 1 + neighbours_x)

    def send_segments(step, carry):
        peer = lax.rem(slab + step, n)
        pltpu.make_async_remote_copy(
            seg_send.at[peer], seg_recv.at[slab], seg_sems.at[0], seg_sems.at[1],
            device_id={"slab": peer}, device_id_type=MESH,
        ).start()
        return carry

    lax.fori_loop(1, n, send_segments, 0)
    seg_recv[slab] = seg_send[slab]

    def halo_copy(index, sweep, sent, landed, target):
        return pltpu.make_async_remote_copy(
            sent.at[sweep], landed.at[sweep],
            halo_send_sems.at[index, sweep], halo_recv_sems.at[index, sweep],
            device_id=target, device_id_type=MESH,
        )

    def halo_copies(sweep):
        above, below = {"slab": slab + 1}, {"slab": slab - 1}
        right, left = {"plane": plane + 1}, {"plane": plane - 1}
        return [
            (has_above, has_below, halo_copy(0, sweep, up_send, up_recv, above)),
            (has_below, has_above, halo_copy(1, sweep, down_send, down_recv, below)),
            (has_right, has_left, halo_copy(2, sweep, right_send, right_recv, right)),
            (has_left, has_right, halo_copy(3, sweep, left_send, left_recv, left)),
            (has_above, has_below, halo_copy(4, sweep, frac_send, below_recv, above)),
            (has_below, has_above, halo_copy(5, sweep, frac_send, above_recv, below)),
        ]

    def start_when(flag, copy):
        @pl.when(flag)
        def _():
            copy.start()

    def landed_when(flag, copy):
        @pl.when(flag)
        def _():
            copy.wait_recv()

    def sent_when(flag, copy):
        @pl.when(flag)
        def _():
            copy.wait_send()

    coef = [[trans_ref[d, z].astype(F32) for z in range(2)] for d in range(3)]
    x_rows = coef[0][0].shape[0]
    width = coef[0][0].shape[1]
    lane = lax.broadcasted_iota(jnp.int32, (x_rows, width), 1)
    row = lax.broadcasted_iota(jnp.int32, (x_rows, width), 0)
    parts_y = width // LANES

    def send_halos(sweep, rock, frac):
        for f in range(2):
            up_send[sweep, f] = rock[f][1]
            down_send[sweep, f] = coef[0][0] * rock[f][0]
            for z in range(2):
                at = slice(f * 2 + z, f * 2 + z + 1)
                right_send[sweep, at] = rock[f][z][x_rows - 1 :]
                left_send[sweep, at] = coef[1][z][:1] * rock[f][z][:1]
        frac_send[sweep] = frac.astype(BF16)
        for sends, _, copy in halo_copies(sweep):
            start_when(sends, copy)

    rock = [[rock_ref[f, z] for z in range(2)] for f in range(2)]

    def to_blocks(ref):
        return jnp.concatenate(
            [ref[f : f + 1, b * LANES : (b + 1) * LANES] for f in range(2) for b in range(blocks)],
            axis=0,
        )

    frac = to_blocks(frac_ref)
    frac_source = to_blocks(frac_source_ref)
    send_halos(0, rock, frac)

    slot_lane = lax.broadcasted_iota(jnp.int32, (1, LANES), 1)
    table_rows = 2 * x_rows * parts_y
    hot_row = lax.broadcasted_iota(jnp.int32, (LANES, LANES), 0)
    mask_row = lax.broadcasted_iota(jnp.int32, (table_rows, LANES), 0)
    block_row = lax.broadcasted_iota(jnp.int32, (blocks, LANES), 0)
    y_shift = width.bit_length() - 1
    for s in range(n):
        at = slice(s * LANES, (s + 1) * LANES)
        cell = cell_ref[0, s : s + 1, :]
        hot = jnp.where(hot_row == (cell & (LANES - 1)), 1.0, 0.0).astype(BF16)
        cell_hot[:LANES, at] = hot
        cell_hot[LANES:, at] = hot
        y_part = (cell & (width - 1)) >> 7
        table_row = y_part * (2 * x_rows) + (cell >> y_shift)
        cell_mask[:, at] = jnp.where(mask_row == table_row, 1.0, 0.0)
        weights[s : s + 1, :] = jnp.where(
            slot_lane < count_ref[0, s], weight_ref[0, s : s + 1, :], 0.0
        )

    def pick_rock(sweep, rock):
        table = jnp.concatenate(
            [
                rock[f][z][:, p * LANES : (p + 1) * LANES]
                for f in range(2) for p in range(parts_y) for z in range(2)
            ],
            axis=0,
        )
        left = jnp.concatenate(split(table), axis=1)
        for c in range(n // 2):
            at = slice(c * 256, (c + 1) * 256)
            spread = jnp.dot(left, cell_hot[:, at], preferred_element_type=F32)
            mask = cell_mask[:, at]
            for f in range(2):
                picked = jnp.sum(
                    spread[f * table_rows : (f + 1) * table_rows] * mask, axis=0, keepdims=True
                )
                for h in range(2):
                    s = 2 * c + h
                    slot_send[sweep, s, f : f + 1] = (
                        picked[:, h * LANES : (h + 1) * LANES] * weights[s : s + 1]
                    )

    def pick_frac(sweep, frac):
        left = jnp.concatenate(split(frac), axis=1)
        for c in range(n // 2):
            at = slice(c * 256, (c + 1) * 256)
            spread = jnp.dot(left, seg_hot[:, at], preferred_element_type=F32)
            mask = seg_mask[:, at]
            for f in range(2):
                picked = jnp.sum(
                    spread[f * blocks : (f + 1) * blocks] * mask, axis=0, keepdims=True
                )
                for h in range(2):
                    slot_send[sweep, 2 * c + h, 2 + f : 3 + f] = picked[
                        :, h * LANES : (h + 1) * LANES
                    ]

    def send_slots(sweep):
        def body(step, carry):
            peer = lax.rem(slab + step, n)
            pltpu.make_async_remote_copy(
                slot_send.at[sweep, peer], slot_recv.at[sweep, slab],
                slot_sems.at[0, sweep], slot_sems.at[1, sweep],
                device_id={"slab": peer}, device_id_type=MESH,
            ).start()
            return carry

        lax.fori_loop(1, n, body, 0)
        slot_recv[sweep, slab] = slot_send[sweep, slab]

    def place(values, mask_ref, hot_ref, count):
        pieces = []
        for s in range(n):
            mask = mask_ref[:, s * LANES : (s + 1) * LANES]
            parts = [split(value) for value in values(s)]
            column = [
                (parts[f][h].astype(F32) * mask).astype(BF16) for h in range(2) for f in range(2)
            ]
            pieces.append(jnp.concatenate(column, axis=0))
        left = jnp.concatenate(pieces, axis=1)
        result = lax.dot_general(left, hot_ref[:LANES, :], NT, preferred_element_type=F32)
        return result[: 2 * count] + result[2 * count :]

    pick_rock(0, rock)

    my_part = slab * planes + plane
    q = lax.broadcasted_iota(jnp.int32, (2 * blocks, 6 * blocks), 1)
    f_row = lax.broadcasted_iota(jnp.int32, (2 * blocks, 6 * blocks), 0) // blocks
    rim = []
    for k in range(3):
        near = near_ref[:, k : k + 1]
        owner = near // blocks
        side = jnp.where(owner > my_part, 2, jnp.where(owner < my_part, 0, 1))
        code = side * (2 * blocks) + near % blocks
        code = jnp.concatenate([code, code], axis=0)
        rim.append(jnp.where(q == code + f_row * blocks, 1.0, 0.0).astype(BF16))
    rim = jnp.concatenate(rim, axis=0)
    block_of_row = lax.broadcasted_iota(jnp.int32, (2 * blocks, LANES), 0) % blocks

    for half, sem in ((seg_send, 0), (seg_recv, 1)):
        pltpu.make_async_copy(
            half.at[pl.ds(0, n - 1)], half.at[pl.ds(0, n - 1)], seg_sems.at[sem]
        ).wait()
    for s in range(n):
        at = slice(s * LANES, (s + 1) * LANES)
        segment = seg_recv[s]
        hot = jnp.where(hot_row == (segment & (LANES - 1)), 1.0, 0.0).astype(BF16)
        seg_hot[:LANES, at] = hot
        seg_hot[LANES:, at] = hot
        seg_mask[:, at] = jnp.where(block_row == (segment >> 7), 1.0, 0.0)

    def by_block(left, right):
        total = jnp.zeros((2 * blocks, LANES), F32)
        for b in range(0, blocks, 2):
            matrices = jnp.concatenate([right(b), right(b + 1)], axis=0)
            result = lax.dot_general(left, matrices, NT, preferred_element_type=F32)
            total = jnp.where(block_of_row == b, result[:, :LANES], total)
            total = jnp.where(block_of_row == b + 1, result[:, LANES:], total)
        return total

    for sweep in range(ITERS):
        if sweep:
            pick_rock(sweep, rock)
        pick_frac(sweep, frac)
        send_slots(sweep)

        near_sum = [[None, None], [None, None]]
        for f in range(2):
            for z in range(2):
                value = rock[f][z]
                product_y = coef[2][z] * value
                product_x = coef[1][z] * value
                total = source_ref[f, z]
                total += coef[2][z] * jnp.where(lane == 0, 0.0, pltpu.roll(value, 1, 1))
                total += jnp.where(lane == width - 1, 0.0, pltpu.roll(product_y, width - 1, 1))
                total += coef[1][z] * jnp.where(row == 0, 0.0, pltpu.roll(value, 1, 0))
                total += jnp.where(
                    row == x_rows - 1, 0.0, pltpu.roll(product_x, x_rows - 1, 0)
                )
                near_sum[f][z] = total
            near_sum[f][0] += coef[0][1] * rock[f][1]
            near_sum[f][1] += coef[0][1] * rock[f][0]

        copies = halo_copies(sweep)
        for _, lands, copy in copies:
            landed_when(lands, copy)
        for f in range(2):
            near_sum[f][0] += coef[0][0] * up_recv[sweep, f]
            near_sum[f][1] += down_recv[sweep, f]
            for z in range(2):
                at = slice(f * 2 + z, f * 2 + z + 1)
                near_sum[f][z] += jnp.where(
                    row == 0, coef[1][z] * right_recv[sweep, at],
                    jnp.where(row == x_rows - 1, left_recv[sweep, at], 0.0),
                )
        around = jnp.concatenate(
            [below_recv[sweep], frac.astype(BF16), above_recv[sweep]], axis=0
        )
        gathered = jnp.dot(rim, around, preferred_element_type=F32).astype(BF16)
        gathered = jnp.concatenate(
            [gathered[k * 2 * blocks : (k + 1) * 2 * blocks] for k in range(3)], axis=1
        )
        coupled = by_block(
            gathered, lambda b: jnp.concatenate([coupling_ref[b, k] for k in range(3)], axis=1)
        )

        pltpu.make_async_copy(
            slot_recv.at[sweep, pl.ds(0, n - 1)], slot_recv.at[sweep, pl.ds(0, n - 1)],
            slot_sems.at[1, sweep],
        ).wait()
        leak_frac = place(
            lambda s: [slot_recv[sweep, s, f : f + 1] for f in range(2)], seg_mask, seg_hot, blocks
        )
        frac_rhs = (frac_source + leak_frac - coupled).astype(BF16)
        frac = by_block(frac_rhs, lambda b: frac_inverse_ref[b])
        leak_rock = place(
            lambda s: [
                weights[s : s + 1] * slot_recv[sweep, s, 2 + f : 3 + f] for f in range(2)
            ],
            cell_mask, cell_hot, table_rows,
        )
        rhs = [[None, None], [None, None]]
        for f in range(2):
            for z in range(2):
                first = [f * table_rows + (p * 2 + z) * x_rows for p in range(parts_y)]
                rhs[f][z] = near_sum[f][z] + jnp.concatenate(
                    [leak_rock[i : i + x_rows] for i in first], axis=1
                )
        rock = [
            [
                inverse_ref[2 * g, z].astype(F32) * rhs[0][z]
                + inverse_ref[2 * g + 1, z].astype(F32) * rhs[1][z]
                for z in range(2)
            ]
            for g in range(2)
        ]
        if sweep < ITERS - 1:
            send_halos(sweep + 1, rock, frac)

    for f in range(2):
        for z in range(2):
            rock_out[f, z] = rock[f][z]
        for b in range(blocks):
            frac_out[f : f + 1, b * LANES : (b + 1) * LANES] = frac[
                f * blocks + b : f * blocks + b + 1
            ]
    for sweep in range(ITERS):
        for sends, _, copy in halo_copies(sweep):
            sent_when(sends, copy)
        pltpu.make_async_copy(
            slot_send.at[sweep, pl.ds(0, n - 1)], slot_send.at[sweep, pl.ds(0, n - 1)],
            slot_sems.at[0, sweep],
        ).wait()


def shards(n, planes, *operands):
    rock_state = operands[0]
    blocks = operands[6].shape[0]
    _, layers, x_rows, width = rock_state.shape
    table_rows = layers * x_rows * width // LANES
    vmem = pl.BlockSpec(memory_space=pltpu.VMEM)
    smem = pl.BlockSpec(memory_space=pltpu.SMEM)
    slots = n * LANES
    return pl.pallas_call(
        functools.partial(kernel, n, planes),
        out_shape=(
            jax.ShapeDtypeStruct(rock_state.shape, F32),
            jax.ShapeDtypeStruct(operands[4].shape, F32),
        ),
        in_specs=[vmem] * 12 + [smem],
        out_specs=(vmem, vmem),
        scratch_shapes=[
            pltpu.VMEM((2 * LANES, slots), BF16),
            pltpu.VMEM((table_rows, slots), F32),
            pltpu.VMEM((2 * LANES, slots), BF16),
            pltpu.VMEM((blocks, slots), F32),
            pltpu.VMEM((n, LANES), F32),
            pltpu.VMEM((n, 1, LANES), jnp.int32),
            pltpu.VMEM((n, 1, LANES), jnp.int32),
            pltpu.VMEM((ITERS, n, 4, LANES), F32),
            pltpu.VMEM((ITERS, n, 4, LANES), F32),
            pltpu.VMEM((ITERS, 2, x_rows, width), F32),
            pltpu.VMEM((ITERS, 2, x_rows, width), F32),
            pltpu.VMEM((ITERS, 2, x_rows, width), F32),
            pltpu.VMEM((ITERS, 2, x_rows, width), F32),
            pltpu.VMEM((ITERS, 2 * layers, width), F32),
            pltpu.VMEM((ITERS, 2 * layers, width), F32),
            pltpu.VMEM((ITERS, 2 * layers, width), F32),
            pltpu.VMEM((ITERS, 2 * layers, width), F32),
            pltpu.VMEM((ITERS, 2 * blocks, LANES), BF16),
            pltpu.VMEM((ITERS, 2 * blocks, LANES), BF16),
            pltpu.VMEM((ITERS, 2 * blocks, LANES), BF16),
            pltpu.SemaphoreType.DMA((2,)),
            pltpu.SemaphoreType.DMA((2, ITERS)),
            pltpu.SemaphoreType.DMA((6, ITERS)),
            pltpu.SemaphoreType.DMA((6, ITERS)),
        ],
        compiler_params=pltpu.CompilerParams(
            collective_id=0, has_side_effects=True, vmem_limit_bytes=48 * 1024 * 1024
        ),
    )(*operands)


def solution(mesh):
    return jax.shard_map(
        functools.partial(shards, mesh.shape["slab"], mesh.shape["plane"]),
        mesh=mesh,
        in_specs=(
            P(None, "slab", "plane", None),
            P(None, "slab", "plane", None),
            P(None, "slab", "plane", None),
            P(None, "slab", "plane", None),
            P(None, ("slab", "plane")),
            P(None, ("slab", "plane")),
            P(("slab", "plane"), None, None, None),
            P(("slab", "plane"), None, None),
            P(("slab", "plane"), None),
            P("slab", "plane", None),
            P("slab", "plane", None),
            P("slab", "plane", None),
            P("slab", "plane"),
        ),
        out_specs=(P(None, "slab", "plane", None), P(None, ("slab", "plane"))),
        check_vma=False,
    )
```

time: 133 us -> 38.8 us (0.29)
  starting transfers between devices: 83 us -> 0 us
  Pallas kernels: 0 us -> 26.7 us
  matrix products: 20 us -> 0 us
  waiting for transfers between devices: 18.4 us -> 0 us
  local copies, waits for them, and re-layouts: 5.27 us -> 10.9 us
  other arithmetic: 4.18 us -> 0 us
    all_to_all x7 -> x0, starting transfers between devices: 46.4 us -> none  [the longest x3 20.9 us: shards(): lax.all_to_all(send_rock, 'slab', split_axis=1, concat_axis=1, tiled=True)]
    ppermute x18 -> x0, starting transfers between devices: 36.6 us -> none  [the longest x12 23.6 us: shifted(): lax.ppermute(value, axis, [(source, source + steps) for source in range(f...]
    pallas_call x0 -> x1, Pallas kernels: none -> 26.7 us  [shards(): pl.pallas_call(functools.partial(kernel, n, planes), out_shape=(jax.Shape...]
    dot_general x20 -> x0, matrix products: 18.2 us -> none  [the longest x6 7.96 us: place_values(): jnp.einsum('kr,fkc->frc', row_onehot, spread, precision=lax.Precision.HIG...]
    all_to_all x7 -> x0, waiting for transfers between devices: 15.5 us -> none  [the longest x3 10.5 us: shards(): lax.all_to_all(send_fracture, 'slab', split_axis=1, concat_axis=1, tiled=...]
    unnamed x24 -> x27, local copies, waits for them, and re-layouts: 0.74 us -> 10.9 us
    ppermute x18 -> x0, waiting for transfers between devices: 2.84 us -> none  [the longest x12 2.82 us: shifted(): lax.ppermute(value, axis, [(source, source + steps) for source in range(f...]
    mul x3 -> x0, local copies, waits for them, and re-layouts: 1.84 us -> none  [shards(): send_rock = slot_weight[None] * rock_picked]
  transfers between devices with their start and end apart: 25 -> 0, of which waited for: 5 -> 0; matrix products, arithmetic and copies ran while one was open for 18% -> 0% of each run, Pallas kernels for 0% -> 0%
where the time goes in v1:
time: 38.8 us; the launch traced here: 38.2 us
  Pallas kernels  26.7 us (69%)
  local copies, waits for them, and re-layouts  10.9 us (28%)
  between operations  0.66 us (2%)
    pallas_call x1, Pallas kernels, shards(): pl.pallas_call(functools.partial(kernel, n, planes), out_shape=(jax.Shape...  26.7 us
    unnamed x27, local copies, waits for them, and re-layouts  10.9 us

profile of v1, /device:TPU:0, one launch (start us, length us, event | category | flops | bytes accessed | tf_op | source)
XLA Modules:
  0.0 38.2 jit_solution(105871263902610853)
XLA Ops:
  0.6 0.0 copy-start.11
  0.6 0.8 %copy.15.near_ref = s32[8,3]{1,0:T(8,128)S(1)} copy(s32[8,3]{0,1:T(4,128)} %param.21) | data formatting | bytes 192 | tf_op args[8]
  1.4 0.0 copy-done.11
  1.4 1.1 %copy-done = bf16[8,3,128,128]{3,2,1,0:T(8,128)(2,1)S(1)} copy-done((bf16[8,3,128,128]{3,2,1,0:T(8,128)(2,1)S(1)}, bf16[8,3,128,128]{3,2,1,0:T(8,128)(2,1)}, u32[]{:S(2)}) %copy-start) | copy-done | bytes 786456
  2.5 0.0 copy-start.1
  2.5 0.9 %copy-done.1 = bf16[8,128,128]{2,1,0:T(8,128)(2,1)S(1)} copy-done((bf16[8,128,128]{2,1,0:T(8,128)(2,1)S(1)}, bf16[8,128,128]{2,1,0:T(8,128)(2,1)}, u32[]{:S(2)}) %copy-start.1) | copy-done | bytes 262168
  3.5 0.0 copy-start.2
  3.5 0.8 %copy-done.2 = f32[2,2,8,512]{3,2,1,0:T(8,128)S(1)} copy-done((f32[2,2,8,512]{3,2,1,0:T(8,128)S(1)}, f32[2,2,8,512]{3,2,1,0:T(8,128)}, u32[]{:S(2)}) %copy-start.2) | copy-done | bytes 65560
  4.3 0.0 copy-start.3
  4.3 0.8 %copy-done.3 = f32[2,2,8,512]{3,2,1,0:T(8,128)S(1)} copy-done((f32[2,2,8,512]{3,2,1,0:T(8,128)S(1)}, f32[2,2,8,512]{3,2,1,0:T(8,128)}, u32[]{:S(2)}) %copy-start.3) | copy-done | bytes 65560
  5.2 0.0 copy-start.4
  5.2 0.8 %copy-done.4 = bf16[4,2,8,512]{3,2,1,0:T(8,128)(2,1)S(1)} copy-done((bf16[4,2,8,512]{3,2,1,0:T(8,128)(2,1)S(1)}, bf16[4,2,8,512]{3,2,1,0:T(8,128)(2,1)}, u32[]{:S(2)}) %copy-start.4) | copy-done | bytes 65560
  6.0 0.0 copy-start.5
  6.0 0.8 %copy-done.5 = bf16[3,2,8,512]{3,2,1,0:T(8,128)(2,1)S(1)} copy-done((bf16[3,2,8,512]{3,2,1,0:T(8,128)(2,1)S(1)}, bf16[3,2,8,512]{3,2,1,0:T(8,128)(2,1)}, u32[]{:S(2)}) %copy-start.5) | copy-done | bytes 49176
  6.8 0.0 copy-start.6
  6.8 0.7 %copy-done.6 = f32[2,1024]{1,0:T(2,128)S(1)} copy-done((f32[2,1024]{1,0:T(2,128)S(1)}, f32[2,1024]{1,0:T(2,128)}, u32[]{:S(2)}) %copy-start.6) | copy-done | bytes 8216
  7.5 0.0 copy-start.7
  7.5 0.7 %copy-done.7 = f32[2,1024]{1,0:T(2,128)S(1)} copy-done((f32[2,1024]{1,0:T(2,128)S(1)}, f32[2,1024]{1,0:T(2,128)}, u32[]{:S(2)}) %copy-start.7) | copy-done | bytes 8216
  8.2 0.7 %copy-done.8 = s32[1,16,128]{2,1,0:T(8,128)S(1)} copy-done((s32[1,16,128]{2,1,0:T(8,128)S(1)}, s32[1,16,128]{2,1,0:T(8,128)}, u32[]{:S(2)}) %copy-start.8) | copy-done | bytes 8216
  8.9 0.7 %copy-done.9 = s32[1,16,128]{2,1,0:T(8,128)S(1)} copy-done((s32[1,16,128]{2,1,0:T(8,128)S(1)}, s32[1,16,128]{2,1,0:T(8,128)}, u32[]{:S(2)}) %copy-start.9) | copy-done | bytes 8216
  9.6 0.7 %copy-done.10 = f32[1,16,128]{2,1,0:T(8,128)S(1)} copy-done((f32[1,16,128]{2,1,0:T(8,128)S(1)}, f32[1,16,128]{2,1,0:T(8,128)}, u32[]{:S(2)}) %copy-start.10) | copy-done | bytes 8216
  10.3 26.7 %shard_map.140 = (f32[2,2,8,512]{3,2,1,0:T(8,128)S(1)}, f32[2,1024]{1,0:T(2,128)S(1)}) custom-call(f32[2,2,8,512]{3,2,1,0:T(8,128)S(1)} %copy-done.2, f32[2,2,8,512]{3,2,1,0:T(8,128)S(1)} %copy-done.3, bf16[3,2,8,512]{3,2,1,0:T(8,128)(2,1)S(1)} %copy-done.5, bf16[4,2,8,512]{3,2,1,0:T(8,128)(2,1)S(1)} %copy-done.4, f32[2,1024]{1,0:T(2,128)S(1)} %copy-done.6, ...), custom_call_target="tpu_custom_call" | custom-call | tf_op jit(solution)/shard_map/pallas_call | solution.py:414
  37.0 0.6 %copy.18 = f32[2,2,8,512]{3,2,1,0:T(8,128)} copy(f32[2,2,8,512]{3,2,1,0:T(8,128)S(1)} %get-tuple-element.4) | data formatting | bytes 131072
  37.6 0.6 %copy.19 = f32[2,1024]{1,0:T(2,128)} copy(f32[2,1024]{1,0:T(2,128)S(1)} %get-tuple-element.5) | data formatting | bytes 16384
  (4 shorter events, 0.0 us)
Async XLA Ops:
  0.6 0.8 %copy-start.11 = (s32[1,16]{1,0:T(1,128)S(1)}, s32[1,16]{1,0:T(1,128)}, u32[]{:S(2)}) copy-start(s32[1,16]{1,0:T(1,128)} %count_ref.1) | copy-start | bytes 196
  1.4 1.1 %copy-start = (bf16[8,3,128,128]{3,2,1,0:T(8,128)(2,1)S(1)}, bf16[8,3,128,128]{3,2,1,0:T(8,128)(2,1)}, u32[]{:S(2)}) copy-start(bf16[8,3,128,128]{3,2,1,0:T(8,128)(2,1)} %coupling_ref.1) | copy-start | bytes 2359300
  2.5 0.9 %copy-start.1 = (bf16[8,128,128]{2,1,0:T(8,128)(2,1)S(1)}, bf16[8,128,128]{2,1,0:T(8,128)(2,1)}, u32[]{:S(2)}) copy-start(bf16[8,128,128]{2,1,0:T(8,128)(2,1)} %frac_inverse_ref.1) | copy-start | bytes 786436
  3.5 0.8 %copy-start.2 = (f32[2,2,8,512]{3,2,1,0:T(8,128)S(1)}, f32[2,2,8,512]{3,2,1,0:T(8,128)}, u32[]{:S(2)}) copy-start(f32[2,2,8,512]{3,2,1,0:T(8,128)} %rock_ref.1) | copy-start | bytes 196612
  4.3 0.8 %copy-start.3 = (f32[2,2,8,512]{3,2,1,0:T(8,128)S(1)}, f32[2,2,8,512]{3,2,1,0:T(8,128)}, u32[]{:S(2)}) copy-start(f32[2,2,8,512]{3,2,1,0:T(8,128)} %source_ref.1) | copy-start | bytes 196612
  5.2 0.8 %copy-start.4 = (bf16[4,2,8,512]{3,2,1,0:T(8,128)(2,1)S(1)}, bf16[4,2,8,512]{3,2,1,0:T(8,128)(2,1)}, u32[]{:S(2)}) copy-start(bf16[4,2,8,512]{3,2,1,0:T(8,128)(2,1)} %inverse_ref.1) | copy-start | bytes 196612
  6.0 0.8 %copy-start.5 = (bf16[3,2,8,512]{3,2,1,0:T(8,128)(2,1)S(1)}, bf16[3,2,8,512]{3,2,1,0:T(8,128)(2,1)}, u32[]{:S(2)}) copy-start(bf16[3,2,8,512]{3,2,1,0:T(8,128)(2,1)} %trans_ref.1) | copy-start | bytes 147460
  6.8 0.7 %copy-start.6 = (f32[2,1024]{1,0:T(2,128)S(1)}, f32[2,1024]{1,0:T(2,128)}, u32[]{:S(2)}) copy-start(f32[2,1024]{1,0:T(2,128)} %frac_ref.1) | copy-start | bytes 24580
  7.5 0.7 %copy-start.7 = (f32[2,1024]{1,0:T(2,128)S(1)}, f32[2,1024]{1,0:T(2,128)}, u32[]{:S(2)}) copy-start(f32[2,1024]{1,0:T(2,128)} %frac_source_ref.1) | copy-start | bytes 24580
  8.2 0.7 %copy-start.8 = (s32[1,16,128]{2,1,0:T(8,128)S(1)}, s32[1,16,128]{2,1,0:T(8,128)}, u32[]{:S(2)}) copy-start(s32[1,16,128]{2,1,0:T(8,128)} %cell_ref.1) | copy-start | bytes 24580
  8.9 0.7 %copy-start.9 = (s32[1,16,128]{2,1,0:T(8,128)S(1)}, s32[1,16,128]{2,1,0:T(8,128)}, u32[]{:S(2)}) copy-start(s32[1,16,128]{2,1,0:T(8,128)} %segment_ref.1) | copy-start | bytes 24580
  9.6 0.7 %copy-start.10 = (f32[1,16,128]{2,1,0:T(8,128)S(1)}, f32[1,16,128]{2,1,0:T(8,128)}, u32[]{:S(2)}) copy-start(f32[1,16,128]{2,1,0:T(8,128)} %weight_ref.1) | copy-start | bytes 24580

commit v2 on v1

--- a/solution.py
+++ b/solution.py
@@ -21,49 +21,60 @@
     return high, low
 
 
-def kernel(
-    n,
-    planes,
-    rock_ref,
-    source_ref,
-    trans_ref,
-    inverse_ref,
-    frac_ref,
-    frac_source_ref,
-    coupling_ref,
-    frac_inverse_ref,
-    near_ref,
-    cell_ref,
-    segment_ref,
-    weight_ref,
-    count_ref,
-    rock_out,
-    frac_out,
-    cell_hot,
-    cell_mask,
-    seg_hot,
-    seg_mask,
-    weights,
-    seg_send,
-    seg_recv,
-    slot_send,
-    slot_recv,
-    up_send,
-    down_send,
-    up_recv,
-    down_recv,
-    right_send,
-    left_send,
-    right_recv,
-    left_recv,
-    frac_send,
-    below_recv,
-    above_recv,
-    seg_sems,
-    slot_sems,
-    halo_send_sems,
-    halo_recv_sems,
-):
+def kernel(n, planes, *refs):
+    arrays, (rock_out, frac_out), held = refs[:13], refs[13:15], refs[15:28]
+    (
+        cell_hot,
+        cell_mask,
+        seg_hot,
+        seg_mask,
+        weights,
+        seg_send,
+        seg_recv,
+        slot_send,
+        slot_recv,
+        up_send,
+        down_send,
+        up_recv,
+        down_recv,
+        right_send,
+        left_send,
+        right_recv,
+        left_recv,
+        frac_send,
+        below_recv,
+        above_recv,
+        seg_sems,
+        slot_sems,
+        halo_send_sems,
+        halo_recv_sems,
+        load_sems,
+    ) = refs[28:]
+    (
+        rock_ref,
+        source_ref,
+        trans_ref,
+        inverse_ref,
+        frac_ref,
+        frac_source_ref,
+        coupling_ref,
+        frac_inverse_ref,
+        near_ref,
+        cell_ref,
+        segment_ref,
+        weight_ref,
+        count_ref,
+    ) = held
+    loads = [
+        pltpu.make_async_copy(arrays[i], held[i], load_sems.at[i]) for i in range(len(arrays))
+    ]
+    for i in (10, 0, 2, 4, 9, 12, 11, 8, 1, 5, 6, 7, 3):
+        loads[i].start()
+
+    def loaded(*which):
+        for i in which:
+            loads[i].wait()
+
     slab = lax.axis_index("slab")
     plane = lax.axis_index("plane")
     blocks = coupling_ref.shape[0]
@@ -88,6 +99,7 @@
     def _():
         pl.semaphore_signal(barrier, inc=1, device_id={"plane": plane + 1}, device_id_type=MESH)
 
+    loaded(10)
     for s in range(n):
         seg_send[s] = segment_ref[0, s : s + 1, :]
 
@@ -157,6 +169,7 @@
         def _():
             copy.wait_send()
 
+    loaded(2, 0, 4)
     coef = [[trans_ref[d, z].astype(F32) for z in range(2)] for d in range(3)]
     x_rows = coef[0][0].shape[0]
     width = coef[0][0].shape[1]
@@ -185,8 +198,8 @@
         )
 
     frac = to_blocks(frac_ref)
-    frac_source = to_blocks(frac_source_ref)
     send_halos(0, rock, frac)
+    loaded(9, 12, 11)
 
     slot_lane = lax.broadcasted_iota(jnp.int32, (1, LANES), 1)
     table_rows = 2 * x_rows * parts_y
@@ -273,18 +286,22 @@
 
     pick_rock(0, rock)
 
+    loaded(8, 5, 1)
+    frac_source = to_blocks(frac_source_ref)
     my_part = slab * planes + plane
-    q = lax.broadcasted_iota(jnp.int32, (2 * blocks, 6 * blocks), 1)
-    f_row = lax.broadcasted_iota(jnp.int32, (2 * blocks, 6 * blocks), 0) // blocks
-    rim = []
+    square = (6 * blocks, 6 * blocks)
+    q = lax.broadcasted_iota(jnp.int32, square, 1)
+    r = lax.broadcasted_iota(jnp.int32, square, 0)
+    code = jnp.zeros(square, jnp.int32)
     for k in range(3):
-        near = near_ref[:, k : k + 1]
-        owner = near // blocks
-        side = jnp.where(owner > my_part, 2, jnp.where(owner < my_part, 0, 1))
-        code = side * (2 * blocks) + near % blocks
-        code = jnp.concatenate([code, code], axis=0)
-        rim.append(jnp.where(q == code + f_row * blocks, 1.0, 0.0).astype(BF16))
-    rim = jnp.concatenate(rim, axis=0)
+        for b in range(blocks):
+            near = near_ref[k, b]
+            owner = near // blocks
+            side = jnp.where(owner > my_part, 2, jnp.where(owner < my_part, 0, 1))
+            for f in range(2):
+                position = side * (2 * blocks) + f * blocks + near % blocks
+                code = jnp.where(r == (2 * k + f) * blocks + b, position, code)
+    rim = jnp.where(q == code, 1.0, 0.0).astype(BF16)
     block_of_row = lax.broadcasted_iota(jnp.int32, (2 * blocks, LANES), 0) % blocks
 
     for half, sem in ((seg_send, 0), (seg_recv, 1)):
@@ -331,6 +348,8 @@
             near_sum[f][0] += coef[0][1] * rock[f][1]
             near_sum[f][1] += coef[0][1] * rock[f][0]
 
+        if sweep == 0:
+            loaded(6, 7, 3)
         copies = halo_copies(sweep)
         for _, lands, copy in copies:
             landed_when(lands, copy)
@@ -404,12 +423,14 @@
 
 
 def shards(n, planes, *operands):
+    operands = operands[:8] + (operands[8].T,) + operands[9:]
     rock_state = operands[0]
     blocks = operands[6].shape[0]
     _, layers, x_rows, width = rock_state.shape
     table_rows = layers * x_rows * width // LANES
     vmem = pl.BlockSpec(memory_space=pltpu.VMEM)
-    smem = pl.BlockSpec(memory_space=pltpu.SMEM)
+    hbm = pl.BlockSpec(memory_space=pltpu.HBM)
+    scalars = (8, 12)
     slots = n * LANES
     return pl.pallas_call(
         functools.partial(kernel, n, planes),
@@ -417,9 +438,13 @@
             jax.ShapeDtypeStruct(rock_state.shape, F32),
             jax.ShapeDtypeStruct(operands[4].shape, F32),
         ),
-        in_specs=[vmem] * 12 + [smem],
+        in_specs=[hbm] * len(operands),
         out_specs=(vmem, vmem),
         scratch_shapes=[
+            (pltpu.SMEM if i in scalars else pltpu.VMEM)(array.shape, array.dtype)
+            for i, array in enumerate(operands)
+        ]
+        + [
             pltpu.VMEM((2 * LANES, slots), BF16),
             pltpu.VMEM((table_rows, slots), F32),
             pltpu.VMEM((2 * LANES, slots), BF16),
@@ -444,9 +469,10 @@
             pltpu.SemaphoreType.DMA((2, ITERS)),
             pltpu.SemaphoreType.DMA((6, ITERS)),
             pltpu.SemaphoreType.DMA((6, ITERS)),
+            pltpu.SemaphoreType.DMA((len(operands),)),
         ],
         compiler_params=pltpu.CompilerParams(
-            collective_id=0, has_side_effects=True, vmem_limit_bytes=48 * 1024 * 1024
+            collective_id=0, has_side_effects=True, vmem_limit_bytes=127 * 512 * 1024
         ),
     )(*operands)
 

time: 38.8 us -> 29.9 us (0.77)
  local copies, waits for them, and re-layouts: 10.9 us -> 2.08 us
    unnamed x27 -> x4, local copies, waits for them, and re-layouts: 10.9 us -> 2.08 us
where the time goes in v2:
time: 29.9 us; the launch traced here: 29.7 us
  Pallas kernels  26.9 us (90%)
  local copies, waits for them, and re-layouts  2.08 us (7%)
  between operations  0.65 us (2%)
    pallas_call x1, Pallas kernels, shards(): pl.pallas_call(functools.partial(kernel, n, planes), out_shape=(jax.Shape...  26.9 us
    unnamed x4, local copies, waits for them, and re-layouts  2.08 us

profile of v2, /device:TPU:0, one launch (start us, length us, event | category | flops | bytes accessed | tf_op | source)
XLA Modules:
  0.0 29.7 jit_solution(10370713281206618792)
XLA Ops:
  0.6 26.9 %shard_map.140 = (f32[2,2,8,512]{3,2,1,0:T(8,128)}, f32[2,1024]{1,0:T(2,128)}) custom-call(f32[2,2,8,512]{3,2,1,0:T(8,128)} %refs_0_.1, f32[2,2,8,512]{3,2,1,0:T(8,128)} %refs_1_.1, bf16[3,2,8,512]{3,2,1,0:T(8,128)(2,1)} %refs_2_.1, bf16[4,2,8,512]{3,2,1,0:T(8,128)(2,1)} %refs_3_.1, f32[2,1024]{1,0:T(2,128)} %refs_4_.1, f32[2,1024]{1,0:T(2,128)} %refs_5_.1, ...), custom_call_target="tpu_custom_call" | custom-call | tf_op jit(solution)/shard_map/pallas_call | solution.py:435
  27.6 0.0 copy-start
  27.6 1.5 %copy.17 = f32[2,2,8,512]{3,2,1,0:T(8,128)} copy(f32[2,2,8,512]{3,2,1,0:T(8,128)} %get-tuple-element.4) | data formatting | bytes 131072
  29.1 0.0 copy-done
  29.1 0.6 %copy.18 = f32[2,1024]{1,0:T(2,128)} copy(f32[2,1024]{1,0:T(2,128)S(1)} %copy-done) | data formatting | bytes 16384
Async XLA Ops:
  27.6 1.5 %copy-start = (f32[2,1024]{1,0:T(2,128)S(1)}, f32[2,1024]{1,0:T(2,128)}, u32[]{:S(2)}) copy-start(f32[2,1024]{1,0:T(2,128)} %get-tuple-element.5) | copy-start | bytes 24580
